TPU v7x, 32 devices: a whole 2x2x4 slice. The times are simulated.
32 devices in a mesh: dp: 8 (over z, y), head: 4 (over x, core).
Axes of the slice: x: 2, y: 2, z: 4, core: 2. Of those that a mesh axis runs over, the one named last changes fastest.
Arguments:
- hidden_in: bfloat16 [2048, 2048], P(('dp', 'head')), may hold values from -6 to 6
- norm_gain: bfloat16 [2048], replicated, may hold values from 0.25 to 1.75
- w_query: bfloat16 [2048, 2048], P(None, 'head'), may hold values from -0.125 to 0.125
- key_weight: bfloat16 [2048, 1024], P(None, 'head'), may hold values from -0.125 to 0.125
- w_value: bfloat16 [2048, 1024], P(None, 'head'), may hold values from -0.125 to 0.125
- query_gain: bfloat16 [128], replicated, may hold values from 0.796875 to 4
- key_gain: bfloat16 [128], replicated, may hold values from 0.25 to 1.75
- w_out: bfloat16 [2048, 2048], P('head'), may hold values from -0.125 to 0.125
- prefix_root_keys: bfloat16 [1024, 1024], P('dp', 'head'), may hold values from -210 to 210
- prefix_root_values: bfloat16 [1024, 1024], P('dp', 'head'), may hold values from -6 to 6
- mid_keys: bfloat16 [4096, 1024], P('dp', 'head'), may hold values from -210 to 210
- mid_values: bfloat16 [4096, 1024], P('dp', 'head'), may hold values from -6 to 6
- mid_lengths: int32 [16], replicated, may hold values from 1 to 256, 2048 in all
- leaf_keys: bfloat16 [4096, 1024], P('dp', 'head'), may hold values from -6 to 6
- leaf_values: bfloat16 [4096, 1024], P('dp', 'head'), may hold values from -6 to 6
- leaf_lengths: int32 [64], P('dp'), may hold values from 1 to 64, 2048 in all
- token_request: int32 [8, 256], P('dp'), may hold values from 0 to 7, never falling along the last dimension, each value on 1 to 64 neighbouring positions
- request_node: int32 [8, 8], P('dp'), may hold values from 0 to 15, as said below
Outputs:
- attn_update: bfloat16 [2048, 2048], P(('dp', 'head'))
- cache_keys: bfloat16 [2048, 1024], P('dp', 'head')
- cache_values: bfloat16 [2048, 1024], P('dp', 'head')
Inputs may be any that keep to these rules, and one draw needn't show every extreme that they name: `token_request`: in each row requests 0 to 7 all occur, in rising order, each on 1 to 64 consecutive tokens; some request has exactly 64. `request_node`: node v is held by dp index v // 2; the 8 requests of one row have parents on 8 different dp indices, one each.
All inputs are finite; a program needn't handle non-finite values. No bound on the sum of `leaf_lengths` on one device may be relied on, other than what follows from the above.
Results may differ from a plain program's by a relative error of at most 0.039.
Values may be sent and summed in bfloat16 or wider, within the bound.
A program may use at most 128 MiB of HBM per device.

v0:
```python
import math
import jax
import jax.numpy as jnp
from jax import lax
from jax.sharding import PartitionSpec as P

MID_DEV = 2
MID_LEN = 256
EPS = 1e-06
THETA = 1000000.0
MASKED = -1e30


def rms_rows(values, gain):
    power = jnp.mean(values * values, axis=-1, keepdims=True)
    return values * lax.rsqrt(power + EPS) * gain


def rotate(values, positions):
    width = values.shape[-1]
    half = width // 2
    exponent = jnp.arange(half).astype(jnp.float32) * (2.0 / width)
    freqs = jnp.power(THETA, -exponent)
    angles = positions.astype(jnp.float32)[:, None] * freqs[None, :]
    cosine = jnp.cos(angles)[:, None, :]
    sine = jnp.sin(angles)[:, None, :]
    first = values[..., :half]
    second = values[..., half:]
    return jnp.concatenate(
        [first * cosine - second * sine, second * cosine + first * sine], axis=-1
    )


def attend_over_block(query_matrix, keys, values, lengths, kv_heads, head_dim):
    blocks, slots, width = query_matrix.shape
    query_group = width // (kv_heads * head_dim)
    span = keys.shape[1]
    heads_query = query_matrix.reshape(blocks, slots, kv_heads, query_group, head_dim)
    key_heads = keys.reshape(blocks, span, kv_heads, head_dim)
    value_heads = values.reshape(blocks, span, kv_heads, head_dim)
    scores = jnp.einsum(
        "bskgd,blkd->bskgl", heads_query, key_heads, preferred_element_type=jnp.float32
    ) / math.sqrt(head_dim)
    live = jnp.arange(span, dtype=jnp.int32)[None, :] < lengths[:, None]
    scores = jnp.where(live[:, None, None, None, :], scores, MASKED)
    highest = jnp.max(scores, axis=-1)
    weights = jnp.exp(scores - highest[..., None])
    total = jnp.sum(weights, axis=-1)
    summed = jnp.einsum(
        "bskgl,blkd->bskgd",
        weights.astype(jnp.bfloat16),
        value_heads,
        preferred_element_type=jnp.float32,
    )
    output = (summed / total[..., None]).astype(jnp.bfloat16).reshape(blocks, slots, width)
    log_total = (highest + jnp.log(total)).reshape(blocks, slots, kv_heads * query_group)
    return (output, log_total)


def body(
    hidden_in,
    norm_gain,
    w_query,
    key_weight,
    w_value,
    query_gain,
    key_gain,
    w_out,
    prefix_root_keys,
    prefix_root_values,
    mid_keys,
    mid_values,
    mid_lengths,
    leaf_keys,
    leaf_values,
    leaf_lengths,
    token_request,
    request_node,
):
    head_dim = query_gain.shape[0]
    query_width = w_query.shape[1]
    key_width = key_weight.shape[1]
    kv_heads = key_width // head_dim
    query_group = query_width // key_width
    scale = 1.0 / math.sqrt(head_dim)
    dp_count = lax.axis_size("dp")
    normalized_input = rms_rows(
        hidden_in.astype(jnp.float32), norm_gain.astype(jnp.float32)
    ).astype(jnp.bfloat16)
    piece = lax.all_gather(normalized_input, "head", axis=0, tiled=True)
    mixed = jnp.concatenate(
        [
            jnp.dot(piece, w_query, preferred_element_type=jnp.float32),
            jnp.dot(piece, key_weight, preferred_element_type=jnp.float32),
            jnp.dot(piece, w_value, preferred_element_type=jnp.float32),
        ],
        axis=1,
    )
    height = mixed.shape[0]
    segment = token_request[0]
    branch_nodes = request_node[0]
    requests = branch_nodes.shape[0]
    request_ids = jnp.arange(requests, dtype=jnp.int32)
    token_ids = jnp.arange(height, dtype=jnp.int32)
    member = segment[None, :] == request_ids[:, None]
    counts = jnp.sum(member.astype(jnp.int32), axis=1)
    starts = jnp.cumsum(counts) - counts
    offset = token_ids - jnp.sum(jnp.where(member, starts[:, None], 0), axis=0)
    node_total = mid_lengths.shape[0]
    node_match = branch_nodes[:, None] == jnp.arange(node_total, dtype=jnp.int32)[None, :]
    branch_length = jnp.sum(jnp.where(node_match, mid_lengths[None, :], 0), axis=1)
    root_total = prefix_root_keys.shape[0] * dp_count
    positions = (
        root_total
        + jnp.sum(jnp.where(member, (branch_length + leaf_lengths)[:, None], 0), axis=0)
        + offset
    )
    query_part = mixed[:, :query_width].reshape(height, query_width // head_dim, head_dim)
    key_portion = mixed[:, query_width : query_width + key_width].reshape(
        height, kv_heads, head_dim
    )
    query_matrix = rotate(rms_rows(query_part, query_gain.astype(jnp.float32)), positions).astype(
        jnp.bfloat16
    )
    new_keys = rotate(rms_rows(key_portion, key_gain.astype(jnp.float32)), positions).astype(
        jnp.bfloat16
    )
    new_values = mixed[:, query_width + key_width :].astype(jnp.bfloat16)
    heads_query = query_matrix.reshape(height, kv_heads, query_group, head_dim)
    query_rows = query_matrix.reshape(height, query_width)
    capacity = 2 * height // dp_count
    slot_ids = jnp.arange(capacity, dtype=jnp.int32)
    req_valid = slot_ids[None, :] < counts[:, None]
    req_picks = jnp.where(req_valid, starts[:, None] + slot_ids[None, :], 0).reshape(-1)
    req_queries = jnp.take(query_rows, req_picks, axis=0).reshape(
        requests, capacity, kv_heads, query_group, head_dim
    )
    req_keys = jnp.take(new_keys, req_picks, axis=0).reshape(requests, capacity, kv_heads, head_dim)
    req_values = jnp.take(new_values, req_picks, axis=0).reshape(
        requests, capacity, kv_heads, head_dim
    )
    leaf_each = leaf_keys.shape[0] // requests
    leaf_heads_key = leaf_keys.reshape(requests, leaf_each, kv_heads, head_dim)
    leaf_heads_value = leaf_values.reshape(requests, leaf_each, kv_heads, head_dim)
    own_live = (slot_ids[None, :] <= slot_ids[:, None])[None, :, :] & req_valid[:, None, :]
    leaf_live = jnp.arange(leaf_each, dtype=jnp.int32)[None, :] < leaf_lengths[:, None]
    own_scores = (
        jnp.einsum("rskgd,rlkd->rskgl", req_queries, req_keys, preferred_element_type=jnp.float32)
        * scale
    )
    leaf_scores = (
        jnp.einsum(
            "rskgd,rlkd->rskgl", req_queries, leaf_heads_key, preferred_element_type=jnp.float32
        )
        * scale
    )
    own_mask = own_live[:, :, None, None, :]
    leaf_mask = leaf_live[:, None, None, None, :]
    own_scores = jnp.where(own_mask, own_scores, MASKED)
    leaf_scores = jnp.where(leaf_mask, leaf_scores, MASKED)
    req_top = jnp.maximum(jnp.max(own_scores, axis=-1), jnp.max(leaf_scores, axis=-1))
    own_weights = jnp.where(own_mask, jnp.exp(own_scores - req_top[..., None]), 0.0)
    leaf_weights = jnp.where(leaf_mask, jnp.exp(leaf_scores - req_top[..., None]), 0.0)
    req_total = jnp.sum(own_weights, axis=-1) + jnp.sum(leaf_weights, axis=-1)
    req_summed = jnp.einsum(
        "rskgl,rlkd->rskgd",
        own_weights.astype(jnp.bfloat16),
        req_values,
        preferred_element_type=jnp.float32,
    )
    req_summed = req_summed + jnp.einsum(
        "rskgl,rlkd->rskgd",
        leaf_weights.astype(jnp.bfloat16),
        leaf_heads_value,
        preferred_element_type=jnp.float32,
    )
    token_slot = jnp.sum(jnp.where(member, (request_ids * capacity)[:, None], 0), axis=0) + offset
    highest = jnp.take(
        req_top.reshape(requests * capacity, kv_heads, query_group), token_slot, axis=0
    )
    total = jnp.take(
        req_total.reshape(requests * capacity, kv_heads, query_group), token_slot, axis=0
    )
    summed = jnp.take(
        req_summed.reshape(requests * capacity, kv_heads, query_group, head_dim), token_slot, axis=0
    )
    piece = (
        lax.all_gather(prefix_root_keys, "dp", axis=0, tiled=True),
        lax.all_gather(prefix_root_values, "dp", axis=0, tiled=True),
    )
    running = total
    gathered = summed
    key_piece = piece[0].reshape(-1, kv_heads, head_dim)
    value_piece = piece[1].reshape(-1, kv_heads, head_dim)
    scores = (
        jnp.einsum("tkgd,skd->tkgs", heads_query, key_piece, preferred_element_type=jnp.float32)
        * scale
    )
    new_top = jnp.maximum(highest, jnp.max(scores, axis=-1))
    shrink = jnp.exp(highest - new_top)
    weights = jnp.exp(scores - new_top[..., None])
    running = running * shrink + jnp.sum(weights, axis=-1)
    gathered = gathered * shrink[..., None] + jnp.einsum(
        "tkgs,skd->tkgd",
        weights.astype(jnp.bfloat16),
        value_piece,
        preferred_element_type=jnp.float32,
    )
    owner_of = branch_nodes // MID_DEV
    owner_ids = jnp.arange(dp_count, dtype=jnp.int32)
    owner_match = owner_of[None, :] == owner_ids[:, None]
    block_start = jnp.sum(jnp.where(owner_match, starts[None, :], 0), axis=1)
    block_count = jnp.sum(jnp.where(owner_match, counts[None, :], 0), axis=1)
    block_slot = jnp.sum(jnp.where(owner_match, (branch_nodes % MID_DEV)[None, :], 0), axis=1)
    block_length = jnp.sum(jnp.where(owner_match, branch_length[None, :], 0), axis=1)
    valid = slot_ids[None, :] < block_count[:, None]
    picks = jnp.where(valid, block_start[:, None] + slot_ids[None, :], 0).reshape(-1)
    query_buffer = jnp.take(query_rows, picks, axis=0).reshape(dp_count, capacity, query_width)
    query_buffer = jnp.where(valid[..., None], query_buffer, jnp.zeros((), jnp.bfloat16))
    wanted = lax.all_to_all(block_slot[:, None], "dp", split_axis=0, concat_axis=0, tiled=True)[
        :, 0
    ]
    own_keys = mid_keys.reshape(MID_DEV, MID_LEN, key_width)
    own_values = mid_values.reshape(MID_DEV, MID_LEN, key_width)
    sent_keys = jnp.take(own_keys, wanted, axis=0)
    sent_values = jnp.take(own_values, wanted, axis=0)
    got_keys, got_values = (
        lax.all_to_all(sent_keys, "dp", split_axis=0, concat_axis=0, tiled=True),
        lax.all_to_all(sent_values, "dp", split_axis=0, concat_axis=0, tiled=True),
    )
    middle_output, middle_log_sum = attend_over_block(
        query_buffer, got_keys, got_values, block_length, kv_heads, head_dim
    )
    flattened_rows = jnp.sum(jnp.where(member, (owner_of * capacity)[:, None], 0), axis=0) + offset
    middle_rows = (
        jnp.take(middle_output.reshape(dp_count * capacity, query_width), flattened_rows, axis=0)
        .astype(jnp.float32)
        .reshape(height, kv_heads, query_group, head_dim)
    )
    middle_maximum = jnp.take(
        middle_log_sum.reshape(dp_count * capacity, kv_heads * query_group), flattened_rows, axis=0
    ).reshape(height, kv_heads, query_group)
    joint = jnp.maximum(new_top, middle_maximum)
    near_part = jnp.exp(new_top - joint)
    far_part = jnp.exp(middle_maximum - joint)
    attn = (near_part[..., None] * gathered + far_part[..., None] * middle_rows) / (
        near_part * running + far_part
    )[..., None]
    attn = attn.reshape(height, query_width).astype(jnp.bfloat16)
    update = lax.psum_scatter(
        jnp.dot(attn, w_out, preferred_element_type=jnp.float32).astype(jnp.bfloat16),
        "head",
        scatter_dimension=0,
        tiled=True,
    )
    return (update, new_keys.reshape(height, key_width), new_values)


def solution(mesh):
    in_specs = (
        P(("dp", "head"), None),
        P(),
        P(None, "head"),
        P(None, "head"),
        P(None, "head"),
        P(),
        P(),
        P("head", None),
        P("dp", "head"),
        P("dp", "head"),
        P("dp", "head"),
        P("dp", "head"),
        P(),
        P("dp", "head"),
        P("dp", "head"),
        P("dp"),
        P("dp", None),
        P("dp", None),
    )
    out_specs = (P(("dp", "head"), None), P("dp", "head"), P("dp", "head"))
    return jax.shard_map(body, mesh=mesh, in_specs=in_specs, out_specs=out_specs, check_vma=False)
```

profile of v0, /device:TPU:0, one launch (start us, length us, event | category | flops | bytes accessed | tf_op | source)
XLA Modules:
  0.0 225.4 jit_solution(1173646855730605797)
XLA Ops:
  7.2 0.9 convert_reduce_fusion
  9.7 0.9 select_reduce_fusion.8
  11.3 7.3 %all-to-all-start = ((s32[8,1,1]{2,1,0:T(1,128)}), s32[8,1,1]{2,1,0:T(1,128)S(1)}, u32[]{:S(2)}, u32[]{:S(2)}) async-start(s32[8,1,1]{2,1,0:T(1,128)} %copy.295), calls=%async_computation | async-start | bytes 8192 | tf_op jit(solution)/shard_map/all_to_all | solution.py:220
  18.7 1.1 fusion.44
  19.8 0.7 convert_element_type.80
  20.5 1.8 fusion.46
  22.3 0.7 add.259
  23.0 1.3 iota_compare_fusion.5
  26.5 1.2 convert_element_type.86
  27.8 1.2 convert_element_type.82
  29.6 0.8 select_reduce_fusion
  32.8 0.9 copy.293
  33.8 1.7 reshape.513
  35.5 0.8 reshape.518
  36.3 29.8 %all_gather.10 = bf16[1024,256]{0,1:T(8,128)(2,1)} all-gather(bf16[128,256]{0,1:T(8,128)(2,1)S(1)} %copy.293), channel_id=1, replica_groups=mesh['dp'=8,'head'=4] {'dp'}, dimensions={0}, use_global_device_ids=true | all-gather | bytes 589824 | tf_op jit(solution)/shard_map/all_gather | solution.py:188
  66.0 0.8 broadcast_and_fusion
  67.5 31.3 %all_gather.11 = bf16[1024,256]{1,0:T(8,128)(2,1)S(1)} all-gather(bf16[128,256]{1,0:T(8,128)(2,1)S(1)} %copy-done.17), channel_id=1, replica_groups=mesh['dp'=8,'head'=4] {'dp'}, dimensions={0}, use_global_device_ids=true | all-gather | bytes 589824 | tf_op jit(solution)/shard_map/all_gather | solution.py:189
  98.7 1.2 multiply_cosine_fusion
  99.9 1.1 copy.311
  102.4 2.6 %gather_fusion.7 = bf16[8,256,256]{2,1,0:T(8,128)(2,1)} fusion(bf16[2,256,256]{2,1,0:T(8,128)(2,1)} %bitcast.146, s32[1024]{0:T(1024)S(1)} %pad_clamp_fusion.3), kind=kCustom, calls=%fused_computation.2.clone | custom fusion | bytes 2097184 | tf_op jit(solution)/shard_map/jit(_take)/gather | solution.py:225
  105.0 2.8 %broadcast_select_fusion = (bf16[8,256,256]{2,1,0:T(8,128)(2,1)}, bf16[8,256,256]{2,1,0:T(8,128)(2,1)}) fusion(bf16[8,256,256]{2,1,0:T(8,128)(2,1)S(1)} %gather_fusion.9, pred[8]{0:T(512)(128)(4,1)S(1)} %compare_and_fusion.2, bf16[8,256,256]{2,1,0:T(8,128)(2,1)} %gather_fusion.7), kind=kLoop, calls=%fused_computation.48 | loop fusion | flops 1048576 | bytes 4194312 | tf_op jit(solution)/shard_map/jit(_take)/select_n | solution.py:226
  107.9 4.4 %all-to-all-start.1 = ((bf16[8,256,256]{2,1,0:T(8,128)(2,1)}), bf16[8,256,256]{2,1,0:T(8,128)(2,1)}, u32[]{:S(2)}, u32[]{:S(2)}) async-start(bf16[8,256,256]{2,1,0:T(8,128)(2,1)} %get-tuple-element.34), calls=%async_computation.1 | async-start | bytes 2097152 | tf_op jit(solution)/shard_map/all_to_all | solution.py:228
  112.3 2.6 %fusion.89 = f32[256,512]{1,0:T(8,128)S(1)} fusion(bf16[256,2048]{1,0:T(8,128)(2,1)} %all-gather.2.cloned.1.call-done, bf16[2048,512]{1,0:T(8,128)(2,1)} %param.26), kind=kOutput, calls=%fused_computation.188 | convolution fusion | flops 536870912 | bytes 3670016 | tf_op jit(solution)/shard_map/dot_general | solution.py:93
  116.5 0.7 copy.291
  117.2 1.0 pad_maximum_fusion
  118.2 0.7 copy.292
  119.5 2.6 %gather_fusion.2 = bf16[512,256]{1,0:T(8,128)(2,1)} fusion(bf16[256,256]{1,0:T(8,128)(2,1)S(1)} %convolution_convert_fusion.1, s32[1024]{0:T(1024)S(1)} %pad_clamp_fusion.6), kind=kCustom, calls=%fused_computation.8 | custom fusion | bytes 526336 | tf_op jit(solution)/shard_map/jit(_take)/gather | solution.py:139
  122.0 1.7 gather.42
  123.8 2.5 %multiply_reduce_fusion.1 = (f32[256,2]{0,1:T(2,128)S(1)}, f32[256,256]{0,1:T(8,128)}) fusion(bf16[256,2048]{1,0:T(8,128)(2,1)S(1)} %copy-done.5, bf16[2048,256]{1,0:T(8,128)(2,1)} %param.27), kind=kOutput, calls=%fused_computation.97 | convolution fusion | flops 268566016 | bytes 2361344 | tf_op jit(solution)/shard_map/dot_general | solution.py:94
  126.2 1.1 copy.280
  128.7 2.1 gather_fusion
  130.9 2.0 gather_fusion.8
  132.9 0.9 broadcast_select_fusion.2
  133.9 2.0 reshape.517
  135.9 2.0 gather_fusion.5
  137.9 0.9 broadcast_select_fusion.3
  138.8 1.2 reshape.512
  140.2 2.6 %fusion.88 = (f32[8,64,2,2]{1,3,2,0:T(2,128)S(1)}, f32[8,64,2,2,64]{1,4,3,2,0:T(8,128)}) fusion(bf16[8,64,2,128,1]{3,2,1,0,4:T(2,128)(2,1)} %bitcast.161, bf16[8,64,2,2,128]{4,3,2,1,0:T(2,128)(2,1)S(1)} %reshape.512, pred[8,64]{1,0:T(8,128)(4,1)S(1)} %copy-done.21), kind=kOutput, calls=%fused_computation.187 | convolution fusion | flops 33945600 | bytes 1319424 | tf_op jit(solution)/shard_map/rskgd,rlkd->rskgl/dot_general | solution.py:152
  142.8 1.7 fusion.87
  144.6 1.1 copy.332
  145.6 1.3 convolution_bitcast_fusion.2
  147.6 1.8 copy.309
  149.4 3.4 %gather_fusion.3 = f32[256,2,2,128]{3,2,1,0:T(2,128)} fusion(f32[512,2,2,128]{3,2,1,0:T(2,128)} %copy.309, s32[1024]{0:T(1024)} %pad_clamp_fusion), kind=kCustom, calls=%fused_computation.9 | custom fusion | bytes 1049600 | tf_op jit(solution)/shard_map/jit(_take)/gather | solution.py:184
  152.8 2.0 copy.310
  154.8 5.7 %all-to-all-start.2 = ((bf16[8,256,256]{2,1,0:T(8,128)(2,1)}), bf16[8,256,256]{2,1,0:T(8,128)(2,1)}, u32[]{:S(2)}, u32[]{:S(2)}) async-start(bf16[8,256,256]{2,1,0:T(8,128)(2,1)} %get-tuple-element.33), calls=%async_computation.2 | async-start | bytes 2097152 | tf_op jit(solution)/shard_map/all_to_all | solution.py:229
  160.8 1.8 fusion.42
  162.9 1.8 gather_fusion.10
  164.7 1.1 copy.317
  165.8 2.2 gather_fusion.6
  168.1 1.8 bitcast_reduce_fusion
  169.9 1.9 copy-done.2
  171.8 0.9 fusion.1
  172.8 1.5 copy.296
  174.3 1.7 bitcast_reduce_fusion.1
  175.9 1.3 copy-done.7
  177.3 0.9 fusion.9
  178.2 1.5 copy.312
  179.7 3.2 %fusion.16 = bf16[8,64,2,2,128]{4,1,3,2,0:T(8,128)(2,1)} fusion(bf16[8,256,2,128,1]{1,3,4,2,0:T(8,128)(2,1)S(1)} %bitcast.158, f32[8,2,256,64,2]{2,3,4,1,0:T(8,128)} %copy-done.7, f32[8,64,2,2]{1,3,2,0:T(2,128)S(1)} %get-tuple-element.47, pred[8,256]{1,0:T(8,128)(4,1)S(1)} %copy-done.19, f32[8,64,2,2]{1,3,2,0:T(2,128)S(1)} %fusion.9), kind=kOutput, calls=%fused_computation.37 | convolution fusion | flops 136839168 | bytes 3688448 | tf_op jit(solution)/shard_map/bskgl,blkd->bskgd/dot_general | solution.py:49
  183.0 1.6 copy.314
  184.8 1.2 gather_fusion.4
  186.2 0.7 gather_fusion.1
  187.1 3.5 %fusion.37 = bf16[256,2,2,128]{0,3,2,1:T(8,128)(2,1)S(1)} fusion(bf16[1024,2,128,1]{0,2,3,1:T(8,128)(2,1)} %bitcast.160, f32[2,256,2,1024]{3,1,2,0:T(8,128)} %copy-done.2, f32[256,2,2]{0,2,1:T(2,128)S(1)} %fusion.74, f32[256,2,2,128]{0,3,2,1:T(8,128)} %copy.310, f32[256,2,2]{0,2,1:T(2,128)S(1)} %get-tuple-element.16, ...), kind=kOutput, calls=%fused_computation.52 | convolution fusion | flops 272891904 | bytes 5788160 | tf_op jit(solution)/shard_map/tkgs,skd->tkgd/dot_general | solution.py:203
  190.7 1.7 convolution_convert_fusion
  193.1 25.5 %reduce-scatter.2.cloned.1.call-done = bf16[64,2048]{1,0:T(8,128)(2,1)} async-done(((bf16[256,2048]{1,0:T(8,128)(2,1)}), bf16[64,2048]{1,0:T(8,128)(2,1)}) %reduce-scatter.2.cloned.1.call-update) | async-done | bytes 262160 | tf_op jit(solution)/shard_map/reduce_scatter | solution.py:250
  (136 shorter events, 16.0 us)
Async XLA Ops:
  7.2 183.5 %copy-start = (bf16[512,2048]{1,0:T(8,128)(2,1)S(1)}, bf16[512,2048]{1,0:T(8,128)(2,1)}, u32[]{:S(2)}) copy-start(bf16[512,2048]{1,0:T(8,128)(2,1)} %param.31) | copy-start | bytes 6291460
  7.2 28.3 %copy-start.16 = (bf16[512,256]{1,0:T(8,128)(2,1)S(1)}, bf16[512,256]{1,0:T(8,128)(2,1)}, u32[]{:S(2)}) copy-start(bf16[512,256]{1,0:T(8,128)(2,1)} %param.38) | copy-start | bytes 786436
  7.2 60.3 %copy-start.17 = (bf16[128,256]{1,0:T(8,128)(2,1)S(1)}, bf16[128,256]{1,0:T(8,128)(2,1)}, u32[]{:S(2)}) copy-start(bf16[128,256]{1,0:T(8,128)(2,1)} %param.33) | copy-start | bytes 196612
  11.3 89.6 %all-to-all-start = ((s32[8,1,1]{2,1,0:T(1,128)}), s32[8,1,1]{2,1,0:T(1,128)S(1)}, u32[]{:S(2)}, u32[]{:S(2)}) async-start(s32[8,1,1]{2,1,0:T(1,128)} %copy.295), calls=%async_computation | async-start | bytes 8192 | tf_op jit(solution)/shard_map/all_to_all | solution.py:220
  18.6 93.7 %all-gather.2.cloned.1.call-start = ((), (), s32[]{:S(2)}) async-start(), calls=%async_computation.4 | async-start | bytes 1310720 | tf_op jit(solution)/shard_map/all_gather | solution.py:90
  22.3 79.5 %copy-start.3 = (bf16[512,256]{1,0:T(8,128)(2,1)S(1)}, bf16[512,256]{1,0:T(8,128)(2,1)}, u32[]{:S(2)}) copy-start(bf16[512,256]{1,0:T(8,128)(2,1)} %param.35) | copy-start | bytes 786436
  101.2 0.6 copy-start.28
  102.4 2.6 %copy-start.29 = (s32[8]{0:T(128)S(1)}, s32[8]{0:T(128)}, u32[]{:S(2)}) copy-start(s32[8]{0:T(128)} %copy-done.28) | copy-start | bytes 100
  107.9 46.9 %all-to-all-start.1 = ((bf16[8,256,256]{2,1,0:T(8,128)(2,1)}), bf16[8,256,256]{2,1,0:T(8,128)(2,1)}, u32[]{:S(2)}, u32[]{:S(2)}) async-start(bf16[8,256,256]{2,1,0:T(8,128)(2,1)} %get-tuple-element.34), calls=%async_computation.1 | async-start | bytes 2097152 | tf_op jit(solution)/shard_map/all_to_all | solution.py:228
  112.3 3.3 %copy-start.27 = (f32[128]{0:T(128)S(1)}, f32[128]{0:T(128)}, u32[]{:S(2)}) copy-start(f32[128]{0:T(128)} %convert_element_type.86) | copy-start | bytes 1540
  115.0 1.0 copy-start.8
  115.9 3.1 %copy-start.5 = (bf16[256,2048]{1,0:T(8,128)(2,1)S(1)}, bf16[256,2048]{1,0:T(8,128)(2,1)}, u32[]{:S(2)}) copy-start(bf16[256,2048]{1,0:T(8,128)(2,1)} %all-gather.2.cloned.1.call-done) | copy-start | bytes 3145732
  115.9 3.1 %copy-start.13 = (bf16[2048,256]{1,0:T(8,128)(2,1)S(1)}, bf16[2048,256]{1,0:T(8,128)(2,1)}, u32[]{:S(2)}) copy-start(bf16[2048,256]{1,0:T(8,128)(2,1)} %param.28) | copy-start | bytes 3145732
  119.4 6.8 %copy-start.1 = (bf16[256,256]{1,0:T(8,128)(2,1)}, bf16[256,256]{1,0:T(8,128)(2,1)S(1)}, u32[]{:S(2)}) copy-start(bf16[256,256]{1,0:T(8,128)(2,1)S(1)} %convolution_convert_fusion.1) | copy-start | bytes 393220
  122.0 5.5 %copy-start.30 = (f32[128]{0:T(128)S(1)}, f32[128]{0:T(128)}, u32[]{:S(2)}) copy-start(f32[128]{0:T(128)} %convert_element_type.82) | copy-start | bytes 1540
  126.2 4.7 %copy-start.12 = (bf16[256,4,128]{2,1,0:T(4,128)(2,1)S(1)}, bf16[256,4,128]{2,1,0:T(4,128)(2,1)}, u32[]{:S(2)}) copy-start(bf16[256,4,128]{2,1,0:T(4,128)(2,1)} %pad_maximum_fusion) | copy-start | bytes 786436
  130.9 2.0 copy-start.26
  135.9 2.0 copy-start.25
  137.9 2.2 copy-start.11
  137.9 2.2 copy-start.23
  137.9 2.3 %copy-start.21 = (pred[8,64]{1,0:T(8,128)(4,1)S(1)}, pred[8,64]{1,0:T(8,128)(4,1)}, u32[]{:S(2)}) copy-start(pred[8,64]{1,0:T(8,128)(4,1)} %iota_compare_fusion.5) | copy-start | bytes 1540
  140.0 2.8 %copy-start.15 = (bf16[8,64,2,2,128]{4,3,2,1,0:T(2,128)(2,1)}, bf16[8,64,2,2,128]{4,3,2,1,0:T(2,128)(2,1)S(1)}, u32[]{:S(2)}) copy-start(bf16[8,64,2,2,128]{4,3,2,1,0:T(2,128)(2,1)S(1)} %reshape.512) | copy-start | bytes 1572868
  140.0 2.8 %copy-start.14 = (pred[8,64,64]{1,2,0:T(8,128)(4,1)S(1)}, pred[8,64,64]{1,2,0:T(8,128)(4,1)}, u32[]{:S(2)}) copy-start(pred[8,64,64]{1,2,0:T(8,128)(4,1)} %broadcast_and_fusion) | copy-start | bytes 98308
  145.6 1.3 copy-start.4
  145.6 1.3 copy-start.9
  145.6 1.4 copy-start.22
  154.8 23.4 %all-to-all-start.2 = ((bf16[8,256,256]{2,1,0:T(8,128)(2,1)}), bf16[8,256,256]{2,1,0:T(8,128)(2,1)}, u32[]{:S(2)}, u32[]{:S(2)}) async-start(bf16[8,256,256]{2,1,0:T(8,128)(2,1)} %get-tuple-element.33), calls=%async_computation.2 | async-start | bytes 2097152 | tf_op jit(solution)/shard_map/all_to_all | solution.py:229
  160.5 7.6 %copy-start.10 = (bf16[256,4,64]{2,0,1:T(8,128)(2,1)S(1)}, bf16[256,4,64]{2,0,1:T(8,128)(2,1)}, u32[]{:S(2)}) copy-start(bf16[256,4,64]{2,0,1:T(8,128)(2,1)} %copy.291) | copy-start | bytes 393220
  160.5 58.1 %reduce-scatter.2.cloned.1.call-start = ((), (), s32[]{:S(2)}) async-start(), calls=%async_computation.5 | async-start | bytes 1310720 | tf_op jit(solution)/shard_map/reduce_scatter | solution.py:250
  162.6 5.5 %copy-start.6 = (bf16[1024,256]{0,1:T(8,128)(2,1)S(1)}, bf16[1024,256]{0,1:T(8,128)(2,1)}, u32[]{:S(2)}) copy-start(bf16[1024,256]{0,1:T(8,128)(2,1)} %all_gather.10) | copy-start | bytes 1572868
  168.1 1.8 copy-start.20
  169.9 1.9 copy-start.2
  172.7 1.5 copy-start.19
  172.8 1.5 copy-start.31
  175.9 1.3 copy-start.7
  182.9 1.9 copy-start.18
  184.8 2.3 %copy-start.24 = (pred[256]{0:T(512)(128)(4,1)S(1)}, pred[256]{0:T(512)(128)(4,1)}, u32[]{:S(2)}) copy-start(pred[256]{0:T(512)(128)(4,1)} %get-tuple-element.28) | copy-start | bytes 772
Sparse Core Ops, SparseCore 0:
  22.4 18.0 all-gather.1
  192.5 26.0 reduce-scatter.1
where the time goes:
time: 227 us; the launch traced here: 225 us
  blocking collectives  61.1 us (27%)
  local copies, waits for them, and re-layouts  50.7 us (22%)
  other arithmetic  32.1 us (14%)
  waiting for transfers between devices  25.6 us (11%)
  matrix products  23.6 us (10%)
  starting transfers between devices  17.7 us (8%)
  between operations  14.8 us (7%)
    all_gather x1, blocking collectives, body(): lax.all_gather(prefix_root_values, 'dp', axis=0, tiled=True)  31.3 us
    all_gather x1, blocking collectives, body(): lax.all_gather(prefix_root_keys, 'dp', axis=0, tiled=True)  29.8 us
    reduce_scatter x1, waiting for transfers between devices, body(): lax.psum_scatter(jnp.dot(attn, w_out, preferred_element_type=jnp.float32)...  25.5 us
    all_to_all x1, starting transfers between devices, body(): lax.all_to_all(block_slot[:, None], 'dp', split_axis=0, concat_axis=0, ti...  7.28 us
    all_to_all x1, starting transfers between devices, body(): lax.all_to_all(sent_values, 'dp', split_axis=0, concat_axis=0, tiled=True)  5.7 us
    unnamed x67, local copies, waits for them, and re-layouts  5.58 us
    gather x2, local copies, waits for them, and re-layouts, body(): jnp.take(req_summed.reshape(requests * capacity, kv_heads, query_group, h...  5.41 us
  transfers between devices with their start and end apart: 5, of which 1 were waited for; matrix products, arithmetic and copies ran while one was open for 37% of the time, Pallas kernels for 0%

commit v1 on v0

--- a/solution.py
+++ b/solution.py
@@ -9,6 +9,29 @@
 EPS = 1e-06
 THETA = 1000000.0
 MASKED = -1e30
+
+
+def in_blocks(value, dim, devices):
+    dims = value.shape
+    tiles = value.reshape(*dims[:dim], devices, dims[dim] // devices, *dims[dim + 1 :])
+    return jnp.moveaxis(tiles, dim, 0)
+
+
+def joined_along(blocks, dim):
+    lengths = list(blocks.shape[1:])
+    lengths[dim] *= blocks.shape[0]
+    return jnp.moveaxis(blocks, 0, dim).reshape(lengths)
+
+
+def swapped_with_each(x, axis, split_dim, concat_dim):
+    size, place = (lax.axis_size(axis), lax.axis_index(axis))
+    blocks = in_blocks(x, split_dim, size)
+    outs = [blocks[place]]
+    for turn in range(1, size):
+        sent = blocks[place ^ turn]
+        outs.append(lax.ppermute(sent, axis, [(i, i ^ turn) for i in range(size)]))
+    blocks = jnp.stack(outs)[place ^ jnp.arange(size)]
+    return joined_along(blocks, concat_dim)
 
 
 def rms_rows(values, gain):
@@ -225,7 +248,7 @@
     sent_keys = jnp.take(own_keys, wanted, axis=0)
     sent_values = jnp.take(own_values, wanted, axis=0)
     got_keys, got_values = (
-        lax.all_to_all(sent_keys, "dp", split_axis=0, concat_axis=0, tiled=True),
+        swapped_with_each(sent_keys, "dp", 0, 0),
         lax.all_to_all(sent_values, "dp", split_axis=0, concat_axis=0, tiled=True),
     )
     middle_output, middle_log_sum = attend_over_block(

time: 227 us -> 252 us (1.11)
  waiting for transfers between devices: 25.6 us -> 46 us
  starting transfers between devices: 17.7 us -> 24.9 us
    ppermute x0 -> x7, waiting for transfers between devices: none -> 23 us  [swapped_with_each(): outs.append(lax.ppermute(sent, axis, [(i, i ^ turn) for i in range(size)]))]
    ppermute x0 -> x7, starting transfers between devices: none -> 13.1 us  [swapped_with_each(): outs.append(lax.ppermute(sent, axis, [(i, i ^ turn) for i in range(size)]))]
    all_to_all x1 -> x0, starting transfers between devices: 4.42 us -> none  [body(): lax.all_to_all(sent_keys, 'dp', split_axis=0, concat_axis=0, tiled=True)]
    gather x0 -> x2, local copies, waits for them, and re-layouts: none -> 3.13 us  [swapped_with_each(): blocks = jnp.stack(outs)[place ^ jnp.arange(size)]]
    reduce_scatter x1, waiting for transfers between devices: 25.5 us -> 23 us  [body(): lax.psum_scatter(jnp.dot(attn, w_out, preferred_element_type=jnp.float32)...]
    unnamed x67 -> x96, local copies, waits for them, and re-layouts: 5.58 us -> 5.73 us
  transfers between devices with their start and end apart: 5 -> 11, of which waited for: 1 -> 5; matrix products, arithmetic and copies ran while one was open for 37% -> 34% of each run, Pallas kernels for 0% -> 0%
where the time goes in v1:
time: 252 us; the launch traced here: 251 us
  blocking collectives  61.1 us (24%)
  local copies, waits for them, and re-layouts  51.2 us (20%)
  waiting for transfers between devices  46 us (18%)
  other arithmetic  32 us (13%)
  starting transfers between devices  24.9 us (10%)
  matrix products  21.2 us (8%)
  between operations  15 us (6%)
    all_gather x1, blocking collectives, body(): lax.all_gather(prefix_root_values, 'dp', axis=0, tiled=True)  31.3 us
    all_gather x1, blocking collectives, body(): lax.all_gather(prefix_root_keys, 'dp', axis=0, tiled=True)  29.8 us
    reduce_scatter x1, waiting for transfers between devices, body(): lax.psum_scatter(jnp.dot(attn, w_out, preferred_element_type=jnp.float32)...  23 us
    ppermute x7, waiting for transfers between devices, swapped_with_each(): outs.append(lax.ppermute(sent, axis, [(i, i ^ turn) for i in range(size)]))  23 us
    ppermute x7, starting transfers between devices, swapped_with_each(): outs.append(lax.ppermute(sent, axis, [(i, i ^ turn) for i in range(size)]))  13.1 us
    all_to_all x1, starting transfers between devices, body(): lax.all_to_all(block_slot[:, None], 'dp', split_axis=0, concat_axis=0, ti...  7.28 us
    unnamed x96, local copies, waits for them, and re-layouts  5.73 us
  transfers between devices with their start and end apart: 11, of which 5 were waited for; matrix products, arithmetic and copies ran while one was open for 34% of the time, Pallas kernels for 0%

profile of v1, /device:TPU:0, one launch (start us, length us, event | category | flops | bytes accessed | tf_op | source)
XLA Modules:
  0.0 251.3 jit_solution(1909418435959537481)
XLA Ops:
  7.2 0.9 convert_reduce_fusion
  9.0 0.9 select_reduce_fusion.8
  10.7 7.3 %all-to-all-start = ((s32[8,1,1]{2,1,0:T(1,128)}), s32[8,1,1]{2,1,0:T(1,128)S(1)}, u32[]{:S(2)}, u32[]{:S(2)}) async-start(s32[8,1,1]{2,1,0:T(1,128)} %copy.325), calls=%async_computation | async-start | bytes 8192 | tf_op jit(solution)/shard_map/all_to_all | solution.py:243
  18.0 1.1 fusion.44
  19.8 1.8 fusion.46
  22.9 1.3 iota_compare_fusion.5
  26.5 1.2 convert_element_type.86
  27.7 1.1 convert_element_type.82
  29.5 1.0 copy.323
  30.5 1.7 reshape.542
  33.0 29.8 %all_gather.10 = bf16[1024,256]{0,1:T(8,128)(2,1)} all-gather(bf16[128,256]{0,1:T(8,128)(2,1)S(1)} %copy.323), channel_id=1, replica_groups=mesh['dp'=8,'head'=4] {'dp'}, dimensions={0}, use_global_device_ids=true | all-gather | bytes 589824 | tf_op jit(solution)/shard_map/all_gather | solution.py:211
  62.7 31.3 %all_gather.11 = bf16[1024,256]{1,0:T(8,128)(2,1)S(1)} all-gather(bf16[128,256]{1,0:T(8,128)(2,1)S(1)} %copy-done.25), channel_id=1, replica_groups=mesh['dp'=8,'head'=4] {'dp'}, dimensions={0}, use_global_device_ids=true | all-gather | bytes 589824 | tf_op jit(solution)/shard_map/all_gather | solution.py:212
  94.1 1.1 copy.347
  99.2 1.6 gather_fusion.10
  100.9 1.6 gather_fusion.8
  102.5 2.8 %broadcast_select_fusion = (bf16[8,256,256]{2,1,0:T(8,128)(2,1)}, bf16[8,256,256]{2,1,0:T(8,128)(2,1)S(1)}) fusion(bf16[8,256,256]{2,1,0:T(8,128)(2,1)} %gather_fusion.10, pred[8]{0:T(512)(128)(4,1)S(1)} %compare_and_fusion.2, bf16[8,256,256]{2,1,0:T(8,128)(2,1)} %gather_fusion.8), kind=kLoop, calls=%fused_computation.49 | loop fusion | flops 1048576 | bytes 4194312 | tf_op jit(solution)/shard_map/jit(_take)/select_n | solution.py:249
  105.3 4.2 %all-to-all-start.1 = ((bf16[8,256,256]{2,1,0:T(8,128)(2,1)}), bf16[8,256,256]{2,1,0:T(8,128)(2,1)}, u32[]{:S(2)}, u32[]{:S(2)}) async-start(bf16[8,256,256]{2,1,0:T(8,128)(2,1)} %get-tuple-element.40), calls=%async_computation.1 | async-start | bytes 2097152 | tf_op jit(solution)/shard_map/all_to_all | solution.py:252
  109.9 4.5 %collective-permute-start.6 = (bf16[1,256,256]{2,1,0:T(8,128)(2,1)S(1)}, bf16[1,256,256]{2,1,0:T(8,128)(2,1)S(1)}, u32[]{:S(2)}, u32[]{:S(2)}) collective-permute-start(bf16[1,256,256]{2,1,0:T(8,128)(2,1)S(1)} %get-tuple-element.22), channel_id=1, source_target_pairs={{0,28},{4,24},{8,20},{12,16},{16,12},{20,8},{24,4},{28,0},{1,29},{... | collective-permute-start | bytes 393224 | tf_op jit(solution)/shard_map/ppermute | solution.py:32
  115.4 2.2 collective-permute-start.3
  117.6 1.6 collective-permute-start
  119.2 1.2 multiply_cosine_fusion
  120.5 2.7 %collective-permute-done = bf16[1,256,256]{2,1,0:T(8,128)(2,1)S(1)} collective-permute-done((bf16[1,256,256]{2,1,0:T(8,128)(2,1)S(1)}, bf16[1,256,256]{2,1,0:T(8,128)(2,1)S(1)}, u32[]{:S(2)}, u32[]{:S(2)}) %collective-permute-start) | collective-permute-done | bytes 131104 | tf_op jit(solution)/shard_map/ppermute | solution.py:32
  123.7 7.9 %collective-permute-done.1 = bf16[1,256,256]{2,1,0:T(8,128)(2,1)S(1)} collective-permute-done((bf16[1,256,256]{2,1,0:T(8,128)(2,1)S(1)}, bf16[1,256,256]{2,1,0:T(8,128)(2,1)S(1)}, u32[]{:S(2)}, u32[]{:S(2)}) %collective-permute-start.1) | collective-permute-done | bytes 131104 | tf_op jit(solution)/shard_map/ppermute | solution.py:32
  131.6 3.3 %collective-permute-start.2 = (bf16[1,256,256]{2,1,0:T(8,128)(2,1)S(1)}, bf16[1,256,256]{2,1,0:T(8,128)(2,1)S(1)}, u32[]{:S(2)}, u32[]{:S(2)}) collective-permute-start(bf16[1,256,256]{2,1,0:T(8,128)(2,1)S(1)} %get-tuple-element.26), channel_id=1, source_target_pairs={{0,12},{4,8},{8,4},{12,0},{16,28},{20,24},{24,20},{28,16},{1,13},{... | collective-permute-start | bytes 393224 | tf_op jit(solution)/shard_map/ppermute | solution.py:32
  134.9 3.1 %collective-permute-done.2 = bf16[1,256,256]{2,1,0:T(8,128)(2,1)S(1)} collective-permute-done((bf16[1,256,256]{2,1,0:T(8,128)(2,1)S(1)}, bf16[1,256,256]{2,1,0:T(8,128)(2,1)S(1)}, u32[]{:S(2)}, u32[]{:S(2)}) %collective-permute-start.2) | collective-permute-done | bytes 131104 | tf_op jit(solution)/shard_map/ppermute | solution.py:32
  138.0 9.2 %collective-permute-done.3 = bf16[1,256,256]{2,1,0:T(8,128)(2,1)S(1)} collective-permute-done((bf16[1,256,256]{2,1,0:T(8,128)(2,1)S(1)}, bf16[1,256,256]{2,1,0:T(8,128)(2,1)S(1)}, u32[]{:S(2)}, u32[]{:S(2)}) %collective-permute-start.3) | collective-permute-done | bytes 131104 | tf_op jit(solution)/shard_map/ppermute | solution.py:32
  147.3 1.0 copy-done.9
  148.3 1.8 gather_fusion.1
  150.1 1.3 copy.332
  151.4 2.6 %fusion.90 = f32[256,512]{1,0:T(8,128)S(1)} fusion(bf16[256,2048]{1,0:T(8,128)(2,1)} %all-gather.2.cloned.1.call-done, bf16[2048,512]{1,0:T(8,128)(2,1)} %param.26), kind=kOutput, calls=%fused_computation.207 | convolution fusion | flops 536870912 | bytes 3670016 | tf_op jit(solution)/shard_map/dot_general | solution.py:116
  156.3 1.1 pad_maximum_fusion
  158.5 2.6 %gather_fusion.3 = bf16[512,256]{1,0:T(8,128)(2,1)} fusion(bf16[256,256]{1,0:T(8,128)(2,1)S(1)} %convolution_convert_fusion.1, s32[1024]{0:T(1024)S(1)} %pad_clamp_fusion.7), kind=kCustom, calls=%fused_computation.9 | custom fusion | bytes 526336 | tf_op jit(solution)/shard_map/jit(_take)/gather | solution.py:162
  161.1 1.7 gather.46
  162.8 2.5 multiply_reduce_fusion.1
  165.3 1.1 copy.310
  167.8 2.1 gather_fusion
  170.0 2.0 gather_fusion.9
  172.0 1.0 broadcast_select_fusion.2
  173.0 2.0 reshape.545
  175.0 2.2 gather_fusion.6
  177.2 1.0 broadcast_select_fusion.3
  178.2 1.2 reshape.541
  179.6 2.6 %fusion.89 = (f32[8,64,2,2]{1,3,2,0:T(2,128)S(1)}, f32[8,64,2,2,64]{1,4,3,2,0:T(8,128)}) fusion(bf16[8,64,2,128,1]{3,2,1,0,4:T(2,128)(2,1)} %bitcast.193, bf16[8,64,2,2,128]{4,3,2,1,0:T(2,128)(2,1)S(1)} %reshape.541, pred[8,64]{1,0:T(8,128)(4,1)S(1)} %copy-done.33), kind=kOutput, calls=%fused_computation.206 | convolution fusion | flops 33945600 | bytes 1319424 | tf_op jit(solution)/shard_map/rskgd,rlkd->rskgl/dot_general | solution.py:175
  182.2 1.7 fusion.88
  183.9 1.1 copy.368
  185.0 2.5 fusion.42
  189.4 2.2 gather_fusion.4
  191.6 2.2 copy.346
  194.0 1.0 gather_fusion.11
  195.7 1.0 gather_fusion.7
  197.4 2.0 bitcast_reduce_fusion.1
  199.5 1.3 copy-done.8
  200.8 0.9 fusion.9
  203.8 1.5 gather_fusion.2
  205.3 1.0 copy.338
  206.4 0.8 bitcast_reduce_fusion
  207.3 0.9 fusion.1
  208.2 1.0 copy-done.2
  209.2 1.7 copy.348
  211.0 2.3 fusion.16
  214.1 1.3 gather_fusion.5
  215.5 3.5 %fusion.37 = bf16[256,2,2,128]{0,3,2,1:T(8,128)(2,1)S(1)} fusion(bf16[1024,2,128,1]{0,2,3,1:T(8,128)(2,1)} %bitcast.192, f32[2,256,2,1024]{3,1,2,0:T(8,128)} %copy-done.2, f32[256,2,2]{0,2,1:T(2,128)S(1)} %fusion.74, f32[256,2,2,128]{0,3,2,1:T(8,128)} %copy.346, f32[256,2,2]{0,2,1:T(2,128)S(1)} %get-tuple-element.16, ...), kind=kOutput, calls=%fused_computation.53 | convolution fusion | flops 272891904 | bytes 5788160 | tf_op jit(solution)/shard_map/tkgs,skd->tkgd/dot_general | solution.py:226
  219.1 1.7 convolution_convert_fusion
  221.5 23.0 %reduce-scatter.2.cloned.1.call-done = bf16[64,2048]{1,0:T(8,128)(2,1)} async-done(((bf16[256,2048]{1,0:T(8,128)(2,1)}), bf16[64,2048]{1,0:T(8,128)(2,1)}) %reduce-scatter.2.cloned.1.call-update) | async-done | bytes 262160 | tf_op jit(solution)/shard_map/reduce_scatter | solution.py:273
  (180 shorter events, 25.7 us)
Async XLA Ops:
  7.2 211.9 %copy-start = (bf16[512,2048]{1,0:T(8,128)(2,1)S(1)}, bf16[512,2048]{1,0:T(8,128)(2,1)}, u32[]{:S(2)}) copy-start(bf16[512,2048]{1,0:T(8,128)(2,1)} %param.31) | copy-start | bytes 6291460
  7.2 25.0 %copy-start.20 = (bf16[512,256]{1,0:T(8,128)(2,1)S(1)}, bf16[512,256]{1,0:T(8,128)(2,1)}, u32[]{:S(2)}) copy-start(bf16[512,256]{1,0:T(8,128)(2,1)} %param.38) | copy-start | bytes 786436
  7.2 55.6 %copy-start.25 = (bf16[128,256]{1,0:T(8,128)(2,1)S(1)}, bf16[128,256]{1,0:T(8,128)(2,1)}, u32[]{:S(2)}) copy-start(bf16[128,256]{1,0:T(8,128)(2,1)} %param.33) | copy-start | bytes 196612
  10.7 85.2 %all-to-all-start = ((s32[8,1,1]{2,1,0:T(1,128)}), s32[8,1,1]{2,1,0:T(1,128)S(1)}, u32[]{:S(2)}, u32[]{:S(2)}) async-start(s32[8,1,1]{2,1,0:T(1,128)} %copy.325), calls=%async_computation | async-start | bytes 8192 | tf_op jit(solution)/shard_map/all_to_all | solution.py:243
  18.0 133.5 %all-gather.2.cloned.1.call-start = ((), (), s32[]{:S(2)}) async-start(), calls=%async_computation.3 | async-start | bytes 1310720 | tf_op jit(solution)/shard_map/all_gather | solution.py:113
  21.6 74.5 %copy-start.41 = (s32[1,8]{1,0:T(1,128)S(1)}, s32[1,8]{1,0:T(1,128)}, u32[]{:S(2)}) copy-start(s32[1,8]{1,0:T(1,128)} %param.41) | copy-start | bytes 100
  21.6 74.6 %copy-start.39 = (s32[1,256]{1,0:T(1,128)S(1)}, s32[1,256]{1,0:T(1,128)}, u32[]{:S(2)}) copy-start(s32[1,256]{1,0:T(1,128)} %param.40) | copy-start | bytes 3076
  21.6 77.6 %copy-start.3 = (bf16[512,256]{1,0:T(8,128)(2,1)S(1)}, bf16[512,256]{1,0:T(8,128)(2,1)}, u32[]{:S(2)}) copy-start(bf16[512,256]{1,0:T(8,128)(2,1)} %param.35) | copy-start | bytes 786436
  62.7 38.1 %copy-start.4 = (bf16[512,256]{1,0:T(8,128)(2,1)S(1)}, bf16[512,256]{1,0:T(8,128)(2,1)}, u32[]{:S(2)}) copy-start(bf16[512,256]{1,0:T(8,128)(2,1)} %param.34) | copy-start | bytes 786436
  105.3 103.9 %all-to-all-start.1 = ((bf16[8,256,256]{2,1,0:T(8,128)(2,1)}), bf16[8,256,256]{2,1,0:T(8,128)(2,1)}, u32[]{:S(2)}, u32[]{:S(2)}) async-start(bf16[8,256,256]{2,1,0:T(8,128)(2,1)} %get-tuple-element.40), calls=%async_computation.1 | async-start | bytes 2097152 | tf_op jit(solution)/shard_map/all_to_all | solution.py:252
  109.5 134.9 %reduce-scatter.2.cloned.1.call-start = ((), (), s32[]{:S(2)}) async-start(), calls=%async_computation.4 | async-start | bytes 1310720 | tf_op jit(solution)/shard_map/reduce_scatter | solution.py:273
  109.9 37.4 %collective-permute-start.6 = (bf16[1,256,256]{2,1,0:T(8,128)(2,1)S(1)}, bf16[1,256,256]{2,1,0:T(8,128)(2,1)S(1)}, u32[]{:S(2)}, u32[]{:S(2)}) collective-permute-start(bf16[1,256,256]{2,1,0:T(8,128)(2,1)S(1)} %get-tuple-element.22), channel_id=1, source_target_pairs={{0,28},{4,24},{8,20},{12,16},{16,12},{20,8},{24,4},{28,0},{1,29},{... | collective-permute-start | bytes 393224 | tf_op jit(solution)/shard_map/ppermute | solution.py:32
  114.3 33.0 %collective-permute-start.5 = (bf16[1,256,256]{2,1,0:T(8,128)(2,1)S(1)}, bf16[1,256,256]{2,1,0:T(8,128)(2,1)S(1)}, u32[]{:S(2)}, u32[]{:S(2)}) collective-permute-start(bf16[1,256,256]{2,1,0:T(8,128)(2,1)S(1)} %get-tuple-element.23), channel_id=1, source_target_pairs={{0,24},{4,28},{8,16},{12,20},{16,8},{20,12},{24,0},{28,4},{1,25},{... | collective-permute-start | bytes 393224 | tf_op jit(solution)/shard_map/ppermute | solution.py:32
  114.8 32.4 %collective-permute-start.4 = (bf16[1,256,256]{2,1,0:T(8,128)(2,1)S(1)}, bf16[1,256,256]{2,1,0:T(8,128)(2,1)S(1)}, u32[]{:S(2)}, u32[]{:S(2)}) collective-permute-start(bf16[1,256,256]{2,1,0:T(8,128)(2,1)S(1)} %get-tuple-element.24), channel_id=1, source_target_pairs={{0,20},{4,16},{8,28},{12,24},{16,4},{20,0},{24,12},{28,8},{1,21},{... | collective-permute-start | bytes 393224 | tf_op jit(solution)/shard_map/ppermute | solution.py:32
  115.4 31.8 %collective-permute-start.3 = (bf16[1,256,256]{2,1,0:T(8,128)(2,1)S(1)}, bf16[1,256,256]{2,1,0:T(8,128)(2,1)S(1)}, u32[]{:S(2)}, u32[]{:S(2)}) collective-permute-start(bf16[1,256,256]{2,1,0:T(8,128)(2,1)S(1)} %get-tuple-element.25), channel_id=1, source_target_pairs={{0,16},{4,20},{8,24},{12,28},{16,0},{20,4},{24,8},{28,12},{1,17},{... | collective-permute-start | bytes 393224 | tf_op jit(solution)/shard_map/ppermute | solution.py:32
  117.6 5.6 %collective-permute-start = (bf16[1,256,256]{2,1,0:T(8,128)(2,1)S(1)}, bf16[1,256,256]{2,1,0:T(8,128)(2,1)S(1)}, u32[]{:S(2)}, u32[]{:S(2)}) collective-permute-start(bf16[1,256,256]{2,1,0:T(8,128)(2,1)S(1)} %get-tuple-element.28), channel_id=1, source_target_pairs={{0,4},{4,0},{8,12},{12,8},{16,20},{20,16},{24,28},{28,24},{1,5},{5... | collective-permute-start | bytes 393224 | tf_op jit(solution)/shard_map/ppermute | solution.py:32
  123.2 8.5 %collective-permute-start.1 = (bf16[1,256,256]{2,1,0:T(8,128)(2,1)S(1)}, bf16[1,256,256]{2,1,0:T(8,128)(2,1)S(1)}, u32[]{:S(2)}, u32[]{:S(2)}) collective-permute-start(bf16[1,256,256]{2,1,0:T(8,128)(2,1)S(1)} %get-tuple-element.27), channel_id=1, source_target_pairs={{0,8},{4,12},{8,0},{12,4},{16,24},{20,28},{24,16},{28,20},{1,9},{5... | collective-permute-start | bytes 393224 | tf_op jit(solution)/shard_map/ppermute | solution.py:32
  131.6 6.4 %collective-permute-start.2 = (bf16[1,256,256]{2,1,0:T(8,128)(2,1)S(1)}, bf16[1,256,256]{2,1,0:T(8,128)(2,1)S(1)}, u32[]{:S(2)}, u32[]{:S(2)}) collective-permute-start(bf16[1,256,256]{2,1,0:T(8,128)(2,1)S(1)} %get-tuple-element.26), channel_id=1, source_target_pairs={{0,12},{4,8},{8,4},{12,0},{16,28},{20,24},{24,20},{28,16},{1,13},{... | collective-permute-start | bytes 393224 | tf_op jit(solution)/shard_map/ppermute | solution.py:32
  147.3 1.0 copy-start.9
  151.4 3.2 %copy-start.40 = (f32[128]{0:T(128)S(1)}, f32[128]{0:T(128)}, u32[]{:S(2)}) copy-start(f32[128]{0:T(128)} %convert_element_type.86) | copy-start | bytes 1540
  155.0 3.1 %copy-start.6 = (bf16[256,2048]{1,0:T(8,128)(2,1)S(1)}, bf16[256,2048]{1,0:T(8,128)(2,1)}, u32[]{:S(2)}) copy-start(bf16[256,2048]{1,0:T(8,128)(2,1)} %all-gather.2.cloned.1.call-done) | copy-start | bytes 3145732
  155.0 3.1 %copy-start.16 = (bf16[2048,256]{1,0:T(8,128)(2,1)S(1)}, bf16[2048,256]{1,0:T(8,128)(2,1)}, u32[]{:S(2)}) copy-start(bf16[2048,256]{1,0:T(8,128)(2,1)} %param.28) | copy-start | bytes 3145732
  158.5 6.8 %copy-start.1 = (bf16[256,256]{1,0:T(8,128)(2,1)}, bf16[256,256]{1,0:T(8,128)(2,1)S(1)}, u32[]{:S(2)}) copy-start(bf16[256,256]{1,0:T(8,128)(2,1)S(1)} %convolution_convert_fusion.1) | copy-start | bytes 393220
  161.1 5.5 %copy-start.42 = (f32[128]{0:T(128)S(1)}, f32[128]{0:T(128)}, u32[]{:S(2)}) copy-start(f32[128]{0:T(128)} %convert_element_type.82) | copy-start | bytes 1540
  165.3 4.7 %copy-start.15 = (bf16[256,4,128]{2,1,0:T(4,128)(2,1)S(1)}, bf16[256,4,128]{2,1,0:T(4,128)(2,1)}, u32[]{:S(2)}) copy-start(bf16[256,4,128]{2,1,0:T(4,128)(2,1)} %pad_maximum_fusion) | copy-start | bytes 786436
  170.0 2.0 copy-start.38
  175.0 2.2 copy-start.37
  177.2 2.2 copy-start.14
  177.2 2.2 copy-start.35
  177.2 2.4 copy-start.33
  179.4 2.8 %copy-start.19 = (bf16[8,64,2,2,128]{4,3,2,1,0:T(2,128)(2,1)}, bf16[8,64,2,2,128]{4,3,2,1,0:T(2,128)(2,1)S(1)}, u32[]{:S(2)}) copy-start(bf16[8,64,2,2,128]{4,3,2,1,0:T(2,128)(2,1)S(1)} %reshape.541) | copy-start | bytes 1572868
  179.4 2.8 %copy-start.17 = (pred[8,64,64]{1,2,0:T(8,128)(4,1)S(1)}, pred[8,64,64]{1,2,0:T(8,128)(4,1)}, u32[]{:S(2)}) copy-start(pred[8,64,64]{1,2,0:T(8,128)(4,1)} %broadcast_and_fusion) | copy-start | bytes 98308
  185.0 2.5 copy-start.18
  185.0 2.9 %copy-start.5 = (f32[8,64,2,2,64]{1,4,3,2,0:T(8,128)S(1)}, f32[8,64,2,2,64]{1,4,3,2,0:T(8,128)}, u32[]{:S(2)}) copy-start(f32[8,64,2,2,64]{1,4,3,2,0:T(8,128)} %get-tuple-element.53) | copy-start | bytes 1572868
  185.0 2.9 %copy-start.11 = (bf16[8,64,2,128]{3,2,1,0:T(2,128)(2,1)S(1)}, bf16[8,64,2,128]{3,2,1,0:T(2,128)(2,1)}, u32[]{:S(2)}) copy-start(bf16[8,64,2,128]{3,2,1,0:T(2,128)(2,1)} %reshape.546) | copy-start | bytes 786436
  185.0 2.9 %copy-start.34 = (pred[8,64]{1,0:T(8,128)(4,1)S(1)}, pred[8,64]{1,0:T(8,128)(4,1)}, u32[]{:S(2)}) copy-start(pred[8,64]{1,0:T(8,128)(4,1)} %iota_compare_fusion.5) | copy-start | bytes 1540
  188.5 5.2 %copy-start.23 = (f32[8,64,2,2]{1,3,2,0:T(2,128)S(1)}, f32[8,64,2,2]{1,3,2,0:T(2,128)}, u32[]{:S(2)}) copy-start(f32[8,64,2,2]{1,3,2,0:T(2,128)} %get-tuple-element.6) | copy-start | bytes 24580
  188.5 5.2 %copy-start.24 = (f32[8,64,2,2]{1,3,2,0:T(2,128)S(1)}, f32[8,64,2,2]{1,3,2,0:T(2,128)}, u32[]{:S(2)}) copy-start(f32[8,64,2,2]{1,3,2,0:T(2,128)} %get-tuple-element.7) | copy-start | bytes 24580
  188.5 5.5 %copy-start.28 = (s32[1024]{0:T(1024)S(1)}, s32[1024]{0:T(1024)}, u32[]{:S(2)}) copy-start(s32[1024]{0:T(1024)} %pad_clamp_fusion.5) | copy-start | bytes 12292
  191.6 4.2 %copy-start.10 = (f32[8,64,2,2]{3,2,1,0:T(2,128)S(1)}, f32[8,64,2,2]{3,2,1,0:T(2,128)}, u32[]{:S(2)}) copy-start(f32[8,64,2,2]{3,2,1,0:T(2,128)} %copy.368) | copy-start | bytes 24580
  196.7 4.1 %copy-start.29 = (pred[8,256]{1,0:T(8,128)(4,1)S(1)}, pred[8,256]{1,0:T(8,128)(4,1)}, u32[]{:S(2)}) copy-start(pred[8,256]{1,0:T(8,128)(4,1)} %iota_compare_fusion.1) | copy-start | bytes 6148
  199.4 1.3 copy-start.8
  199.5 6.9 %copy-start.7 = (bf16[1024,256]{0,1:T(8,128)(2,1)S(1)}, bf16[1024,256]{0,1:T(8,128)(2,1)}, u32[]{:S(2)}) copy-start(bf16[1024,256]{0,1:T(8,128)(2,1)} %all_gather.10) | copy-start | bytes 1572868
  199.5 6.9 %copy-start.12 = (bf16[256,4,64]{2,0,1:T(8,128)(2,1)S(1)}, bf16[256,4,64]{2,0,1:T(8,128)(2,1)}, u32[]{:S(2)}) copy-start(bf16[256,4,64]{2,0,1:T(8,128)(2,1)} %copy.321) | copy-start | bytes 393220
  199.5 6.9 %copy-start.13 = (bf16[256,4,64]{2,0,1:T(8,128)(2,1)S(1)}, bf16[256,4,64]{2,0,1:T(8,128)(2,1)}, u32[]{:S(2)}) copy-start(bf16[256,4,64]{2,0,1:T(8,128)(2,1)} %copy.322) | copy-start | bytes 393220
  201.7 0.6 copy-start.21
  206.3 0.9 copy-start.26
  206.4 0.9 copy-start.31
  207.2 2.0 copy-start.2
  207.2 1.9 copy-start.27
  207.3 1.9 copy-start.36
  209.2 1.8 copy-start.22
  209.2 1.8 copy-start.30
  213.9 1.6 copy-start.32
Sparse Core Ops, SparseCore 0:
  21.8 18.0 all-gather.1
  220.9 23.5 reduce-scatter.1
